TPU v7x, 128 devices: a whole 4x4x4 slice. The times are simulated.
128 devices in a mesh: blk: 16 (over z, y_lo, core), win: 8 (over y_hi, x).
Axes of the slice: x: 4, y: 4 (y_hi: 2, y_lo: 2; y = y_hi * 2 + y_lo), z: 4, core: 2. Of those that a mesh axis runs over, the one named last changes fastest.
Arguments:
- spectra: bfloat16 [1920, 2, 64, 2048], P('win', None, None, 'blk'), may hold values from -0.76171875 to 0.76171875
- partners: int32 [3, 16], replicated, may hold values from 0 to 15, as said below
Outputs:
- cross: float32 [3, 16, 128, 2, 64, 128], P(None, 'blk', 'win')
Inputs may be any that keep to these rules, and one draw needn't show every extreme that they name: Each row of partners pairs the blocks: partners[r, partners[r, b]] = b and partners[r, b] != b; no two blocks are paired in two different rounds.
All inputs are finite; a program needn't handle non-finite values.
Results may differ from a plain program's by a relative error of at most 0.0003.
Values may be sent and summed in bfloat16 or wider, within the bound.
A program may use at most 192 MiB of HBM per device.

v0:
```python
import jax
import jax.numpy as jnp
from jax import lax
from jax.sharding import PartitionSpec as P


def complex_pair(form, left, right):
    real = jnp.einsum(
        form, left[:, 0], right[:, 0], preferred_element_type=jnp.float32
    ) + jnp.einsum(form, left[:, 1], right[:, 1], preferred_element_type=jnp.float32)
    imag = jnp.einsum(
        form, left[:, 0], right[:, 1], preferred_element_type=jnp.float32
    ) - jnp.einsum(form, left[:, 1], right[:, 0], preferred_element_type=jnp.float32)
    return (real, imag)


def shards(spectra, partners):
    spread = lax.all_to_all(
        spectra[:, :, :, None, :], "blk", split_axis=2, concat_axis=3, tiled=True
    )
    results = []
    for step in range(partners.shape[0]):
        mates = jnp.take(spread, partners[step], axis=3)
        real, imag = complex_pair("wfba,wfbc->abfc", spread, mates)
        share = lax.psum_scatter(jnp.stack([real, imag], 2), "win", scatter_dimension=0, tiled=True)
        moved = lax.all_to_all(share, "blk", split_axis=1, concat_axis=3, tiled=True)
        results.append(moved.reshape((1,) + moved.shape[:1] + moved.shape[2:]))
    return jnp.stack(results, 0)


def solution(mesh):
    return jax.shard_map(
        shards,
        mesh=mesh,
        in_specs=(P("win", None, None, "blk"), P()),
        out_specs=P(None, "blk", "win", None, None, None),
        check_vma=False,
    )
```

profile of v0, /device:TPU:1, one launch (start us, length us, event | category | flops | bytes accessed | tf_op | source)
XLA Modules:
  0.0 575.7 jit_solution(2972280605915052229)
XLA Ops:
  6.5 15.5 %copy.28 = bf16[240,2,64,128]{3,1,0,2:T(2,128)(2,1)} copy(bf16[240,2,64,128]{3,2,1,0:T(8,128)(2,1)} %param.4) | data formatting | bytes 15728640 | tf_op args[0]
  22.0 8.0 %all-to-all-start = ((bf16[240,2,64,1,128]{4,1,0,3,2:T(2,128)(2,1)}), bf16[240,2,64,1,128]{4,1,0,3,2:T(2,128)(2,1)}, u32[]{:S(2)}, u32[]{:S(2)}) async-start(bf16[240,2,64,1,128]{4,1,0,3,2:T(2,128)(2,1)} %bitcast.133), calls=%async_computation | async-start | bytes 15728640 | tf_op jit(solution)/shard_map/all_to_all | solution.py:18
  30.1 88.9 %all-to-all-done = bf16[240,2,64,1,128]{4,1,0,3,2:T(2,128)(2,1)} async-done(((bf16[240,2,64,1,128]{4,1,0,3,2:T(2,128)(2,1)}), bf16[240,2,64,1,128]{4,1,0,3,2:T(2,128)(2,1)}, u32[]{:S(2)}, u32[]{:S(2)}) %all-to-all-start) | async-done | bytes 7864352 | tf_op jit(solution)/shard_map/all_to_all | solution.py:18
  119.0 7.3 %copy.16 = bf16[240,2,64,1,128]{4,0,2,1,3:T(8,128)(2,1)} copy(bf16[240,2,64,1,128]{4,1,0,3,2:T(2,128)(2,1)} %all-to-all-done) | data formatting | bytes 15728640 | tf_op jit(solution)/shard_map/all_to_all | solution.py:18
  126.3 7.8 %gather_fusion.2 = bf16[16,240,2,4,128]{4,1,3,2,0:T(8,128)(2,1)} fusion(bf16[240,2,4,16,128]{4,0,2,3,1:T(8,128)(2,1)} %bitcast.114, s32[1024]{0:T(1024)S(1)} %get-tuple-element.16), kind=kCustom, calls=%fused_computation.2.clone | custom fusion | bytes 15728704 | tf_op jit(solution)/shard_map/jit(_take)/gather | solution.py:23
  134.1 7.3 %select_bitcast_fusion = bf16[240,2,4,16,128]{4,0,2,1,3:T(8,128)(2,1)} fusion(bf16[16,240,2,4,128]{4,1,3,2,0:T(8,128)(2,1)} %gather_fusion.2, pred[16]{0:T(512)(128)(4,1)S(1)} %get-tuple-element.12), kind=kLoop, calls=%fused_computation.7 | loop fusion | flops 3932160 | bytes 15728656 | tf_op jit(solution)/shard_map/jit(_take)/select_n | solution.py:23
  141.4 5.7 fusion.8
  148.6 5.7 subtract_bitcast_fusion
  157.7 7.8 %pad_maximum_fusion.2 = f32[128,16,2,4,128]{0,4,3,1,2:T(8,128)} fusion(f32[128,16,1,4,128]{0,4,3,1,2:T(8,128)} %subtract_bitcast_fusion, f32[128,16,1,4,128]{0,4,3,1,2:T(8,128)} %add_bitcast_fusion), kind=kLoop, calls=%fused_computation.5 | loop fusion | flops 2097152 | bytes 16777216 | tf_op jit(solution)/shard_map/stack | solution.py:25
  165.5 10.3 %copy.23 = f32[128,16,2,4,128]{4,1,3,2,0:T(8,128)} copy(f32[128,16,2,4,128]{0,4,3,1,2:T(8,128)} %pad_maximum_fusion.2) | data formatting | bytes 16777216 | tf_op jit(solution)/shard_map/stack | solution.py:25
  176.1 7.8 %gather_fusion.1 = bf16[16,240,2,4,128]{4,1,3,2,0:T(8,128)(2,1)} fusion(bf16[240,2,4,16,128]{4,0,2,3,1:T(8,128)(2,1)} %bitcast.115, s32[1024]{0:T(1024)S(1)} %get-tuple-element.17), kind=kCustom, calls=%fused_computation.1.clone | custom fusion | bytes 15728704 | tf_op jit(solution)/shard_map/jit(_take)/gather | solution.py:23
  183.9 4.8 select_bitcast_fusion.1
  188.7 5.7 fusion.4
  194.4 3.8 fusion.5
  198.3 5.7 subtract_bitcast_fusion.1
  204.0 3.5 add_bitcast_fusion.1
  207.4 8.3 %pad_maximum_fusion.1 = f32[128,16,2,4,128]{0,4,3,1,2:T(8,128)} fusion(f32[128,16,1,4,128]{0,4,3,1,2:T(8,128)} %subtract_bitcast_fusion.1, f32[128,16,1,4,128]{0,4,3,1,2:T(8,128)} %add_bitcast_fusion.1), kind=kLoop, calls=%fused_computation.4 | loop fusion | flops 2097152 | bytes 16777216 | tf_op jit(solution)/shard_map/stack | solution.py:25
  215.7 10.4 %copy.20 = f32[128,16,2,4,128]{4,1,3,2,0:T(8,128)} copy(f32[128,16,2,4,128]{0,4,3,1,2:T(8,128)} %pad_maximum_fusion.1) | data formatting | bytes 16777216 | tf_op jit(solution)/shard_map/stack | solution.py:25
  226.4 7.9 %gather_fusion = bf16[16,240,2,4,128]{4,1,3,2,0:T(8,128)(2,1)} fusion(bf16[240,2,4,16,128]{4,0,2,3,1:T(8,128)(2,1)} %bitcast.118, s32[1024]{0:T(1024)S(1)} %pad_clamp_fusion.2), kind=kCustom, calls=%fused_computation.clone | custom fusion | bytes 15728704 | tf_op jit(solution)/shard_map/jit(_take)/gather | solution.py:23
  234.3 4.2 select_bitcast_fusion.2
  238.6 5.9 %fusion = f32[16,4,128,128]{3,2,1,0:T(8,128)} fusion(bf16[240,2,4,16,128]{4,0,2,1,3:T(8,128)(2,1)S(1)} %select_bitcast_fusion.2, bf16[240,2,4,16,128]{4,0,2,3,1:T(8,128)(2,1)} %bitcast.119), kind=kOutput, calls=%fused_computation.24 | convolution fusion | flops 503316480 | bytes 12058624 | tf_op jit(solution)/shard_map/wfba,wfbc->abfc/dot_general | solution.py:13
  244.5 3.8 fusion.1
  248.3 5.8 %subtract_bitcast_fusion.2 = f32[128,16,1,4,128]{0,4,3,1,2:T(8,128)} fusion(f32[16,4,128,128]{3,2,1,0:T(8,128)} %fusion, bf16[240,2,4,16,128]{4,0,2,1,3:T(8,128)(2,1)S(1)} %select_bitcast_fusion.2, bf16[240,2,4,16,128]{4,0,2,3,1:T(8,128)(2,1)S(1)} %bitcast.131), kind=kOutput, calls=%fused_computation.14 | convolution fusion | flops 504365056 | bytes 16252928 | tf_op jit(solution)/shard_map/wfba,wfbc->abfc/dot_general | solution.py:11
  257.5 8.1 %pad_maximum_fusion = f32[128,16,2,4,128]{0,4,3,1,2:T(8,128)} fusion(f32[128,16,1,4,128]{0,4,3,1,2:T(8,128)} %subtract_bitcast_fusion.2, f32[128,16,1,4,128]{0,4,3,1,2:T(8,128)} %add_bitcast_fusion.2), kind=kLoop, calls=%fused_computation.3 | loop fusion | flops 2097152 | bytes 16777216 | tf_op jit(solution)/shard_map/stack | solution.py:25
  265.6 10.4 %copy.17 = f32[128,16,2,4,128]{4,1,3,2,0:T(8,128)} copy(f32[128,16,2,4,128]{0,4,3,1,2:T(8,128)} %pad_maximum_fusion) | data formatting | bytes 16777216 | tf_op jit(solution)/shard_map/stack | solution.py:25
  276.0 13.7 %reduce-scatter.8.cloned.1.call-done = f32[16,16,2,4,128]{4,1,3,2,0:T(8,128)} async-done(((f32[128,16,2,4,128]{4,1,3,2,0:T(8,128)}), f32[16,16,2,4,128]{4,1,3,2,0:T(8,128)}) %reduce-scatter.8.cloned.1.call-update) | async-done | bytes 1048592 | tf_op jit(solution)/shard_map/reduce_scatter | solution.py:25
  292.5 5.7 all-to-all-start.3
  298.2 117.2 %reduce-scatter.6.cloned.1.call-done = f32[16,16,2,4,128]{4,1,3,2,0:T(8,128)} async-done(((f32[128,16,2,4,128]{4,1,3,2,0:T(8,128)}), f32[16,16,2,4,128]{4,1,3,2,0:T(8,128)}) %reduce-scatter.6.cloned.1.call-update) | async-done | bytes 1048592 | tf_op jit(solution)/shard_map/reduce_scatter | solution.py:25
  418.2 5.6 all-to-all-start.2
  423.8 116.8 %reduce-scatter.4.cloned.1.call-done = f32[16,16,2,4,128]{4,1,3,2,0:T(8,128)} async-done(((f32[128,16,2,4,128]{4,1,3,2,0:T(8,128)}), f32[16,16,2,4,128]{4,1,3,2,0:T(8,128)}) %reduce-scatter.4.cloned.1.call-update) | async-done | bytes 1048592 | tf_op jit(solution)/shard_map/reduce_scatter | solution.py:25
  543.5 5.6 all-to-all-start.1
  551.2 13.7 %all-to-all-done.1 = f32[16,16,2,4,128]{4,0,3,2,1:T(8,128)S(1)} async-done(((f32[16,16,2,4,128]{4,0,3,2,1:T(8,128)}), f32[16,16,2,4,128]{4,0,3,2,1:T(8,128)S(1)}, u32[]{:S(2)}, u32[]{:S(2)}) %all-to-all-start.1) | async-done | bytes 1048608 | tf_op jit(solution)/shard_map/all_to_all | solution.py:26
  (40 shorter events, 23.7 us)
Async XLA Ops:
  22.0 8.0 %copy-start.3 = (s32[3,16]{1,0:T(4,128)S(1)}, s32[3,16]{1,0:T(4,128)}, u32[]{:S(2)}) copy-start(s32[3,16]{1,0:T(4,128)} %param.5) | copy-start | bytes 580
  22.0 97.0 %all-to-all-start = ((bf16[240,2,64,1,128]{4,1,0,3,2:T(2,128)(2,1)}), bf16[240,2,64,1,128]{4,1,0,3,2:T(2,128)(2,1)}, u32[]{:S(2)}, u32[]{:S(2)}) async-start(bf16[240,2,64,1,128]{4,1,0,3,2:T(2,128)(2,1)} %bitcast.133), calls=%async_computation | async-start | bytes 15728640 | tf_op jit(solution)/shard_map/all_to_all | solution.py:18
  30.0 259.7 %reduce-scatter.8.cloned.1.call-start = ((), (), s32[]{:S(2)}) async-start(), calls=%async_computation.9 | async-start | bytes 9437184 | tf_op jit(solution)/shard_map/reduce_scatter | solution.py:25
  134.1 7.3 %copy-start = (bf16[240,2,64,1,128]{4,0,2,1,3:T(8,128)(2,1)S(1)}, bf16[240,2,64,1,128]{4,0,2,1,3:T(8,128)(2,1)}, u32[]{:S(2)}) copy-start(bf16[240,2,64,1,128]{4,0,2,1,3:T(8,128)(2,1)} %copy.16) | copy-start | bytes 23592964
  141.4 5.7 copy-start.1
  175.8 239.5 %reduce-scatter.6.cloned.1.call-start = ((), (), s32[]{:S(2)}) async-start(), calls=%async_computation.8 | async-start | bytes 9437184 | tf_op jit(solution)/shard_map/reduce_scatter | solution.py:25
  188.7 9.6 %slice-start = ((s8[7864320]{0:T(1024)(128)(4,1)}), s8[4194304]{0:T(1024)(128)(4,1)S(1)}, s32[]{:S(2)}) async-start(s8[7864320]{0:T(1024)(128)(4,1)} %bitcast.125), calls=%async_computation.10 | async-start | bytes 8388608
  194.4 3.8 slice-start.1
  226.1 314.5 %reduce-scatter.4.cloned.1.call-start = ((), (), s32[]{:S(2)}) async-start(), calls=%async_computation.7 | async-start | bytes 9437184 | tf_op jit(solution)/shard_map/reduce_scatter | solution.py:25
  238.6 9.7 %slice-start.2 = ((s8[7864320]{0:T(1024)(128)(4,1)}), s8[4194304]{0:T(1024)(128)(4,1)S(1)}, s32[]{:S(2)}) async-start(s8[7864320]{0:T(1024)(128)(4,1)} %bitcast.129), calls=%async_computation.12 | async-start | bytes 8388608
  244.5 3.8 slice-start.3
  292.5 125.7 %all-to-all-start.3 = ((f32[16,16,2,4,128]{4,0,3,2,1:T(8,128)}), f32[16,16,2,4,128]{4,0,3,2,1:T(8,128)S(1)}, u32[]{:S(2)}, u32[]{:S(2)}) async-start(f32[16,16,2,4,128]{4,0,3,2,1:T(8,128)} %copy.24), calls=%async_computation.6 | async-start | bytes 2097152 | tf_op jit(solution)/shard_map/all_to_all | solution.py:26
  418.2 125.3 %all-to-all-start.2 = ((f32[16,16,2,4,128]{4,0,3,2,1:T(8,128)}), f32[16,16,2,4,128]{4,0,3,2,1:T(8,128)S(1)}, u32[]{:S(2)}, u32[]{:S(2)}) async-start(f32[16,16,2,4,128]{4,0,3,2,1:T(8,128)} %copy.21), calls=%async_computation.4 | async-start | bytes 2097152 | tf_op jit(solution)/shard_map/all_to_all | solution.py:26
  543.5 21.5 %all-to-all-start.1 = ((f32[16,16,2,4,128]{4,0,3,2,1:T(8,128)}), f32[16,16,2,4,128]{4,0,3,2,1:T(8,128)S(1)}, u32[]{:S(2)}, u32[]{:S(2)}) async-start(f32[16,16,2,4,128]{4,0,3,2,1:T(8,128)} %copy.18), calls=%async_computation.2 | async-start | bytes 2097152 | tf_op jit(solution)/shard_map/all_to_all | solution.py:26
  550.2 14.9 %copy-start.2 = (f32[16,16,2,4,128]{4,0,3,1,2:T(8,128)S(1)}, f32[16,16,2,4,128]{4,0,3,1,2:T(8,128)}, u32[]{:S(2)}) copy-start(f32[16,16,2,4,128]{4,0,3,1,2:T(8,128)} %copy.25) | copy-start | bytes 3145732
Sparse Core Ops, SparseCore 0:
  176.0 113.7 reduce-scatter.7
  293.6 121.7 reduce-scatter.5
  419.3 121.3 reduce-scatter.3
where the time goes:
time: 577 us; the launch traced here: 576 us
  waiting for transfers between devices  350 us (61%)
  local copies, waits for them, and re-layouts  90.7 us (16%)
  matrix products  53.9 us (9%)
  other arithmetic  42 us (7%)
  starting transfers between devices  25.5 us (4%)
  between operations  13.3 us (2%)
    reduce_scatter x3, waiting for transfers between devices, shards(): lax.psum_scatter(jnp.stack([real, imag], 2), 'win', scatter_dimension=0,...  248 us
    all_to_all x1, waiting for transfers between devices, shards(): lax.all_to_all(spectra[:, :, :, None, :], 'blk', split_axis=2, concat_axi...  88.9 us
    another operation x3, local copies, waits for them, and re-layouts, shards(): jnp.stack([real, imag], 2)  31.1 us
    another operation x3, other arithmetic, shards(): jnp.stack([real, imag], 2)  24.2 us
    gather x3, local copies, waits for them, and re-layouts, shards(): mates = jnp.take(spread, partners[step], axis=3)  23.5 us
    dot_general x3, matrix products, complex_pair(): jnp.einsum(form, left[:, 1], right[:, 0], preferred_element_type=jnp.floa...  17.4 us
    dot_general x3, matrix products, complex_pair(): jnp.einsum(form, left[:, 0], right[:, 1], preferred_element_type=jnp.floa...  17.2 us
    all_to_all x3, starting transfers between devices, shards(): lax.all_to_all(share, 'blk', split_axis=1, concat_axis=3, tiled=True)  17 us
  transfers between devices with their start and end apart: 7, of which 5 were waited for; matrix products, arithmetic and copies ran while one was open for 19% of the time, Pallas kernels for 0%

commit v1 on v0

v1 whole, which is shorter than its diff:
```python
import jax
import jax.numpy as jnp
from jax import lax
from jax.experimental import pallas as pl
from jax.experimental.pallas import tpu as pltpu
from jax.sharding import Mesh, PartitionSpec as P


def cross_kernel(mates, x_ref, p_ref, o_ref):
    def wide(ref):
        v = ref[0]
        rows = v.shape[0] * v.shape[2]
        return jnp.concatenate(
            [v[:, 0].reshape(rows, v.shape[3]), v[:, 1].reshape(rows, v.shape[3])], axis=1
        )

    left, right = wide(x_ref), wide(p_ref)
    g = lax.dot_general(
        left, right, (((0,), (0,)), ((), ())), preferred_element_type=jnp.float32
    )
    n = x_ref.shape[-1]
    real = g[:n, :n] + g[n:, n:]
    imag = g[:n, n:] - g[n:, :n]
    o_ref[0, :, 0, :, 0, :] = real.reshape(o_ref.shape[1], o_ref.shape[3], n)
    o_ref[0, :, 0, :, 1, :] = imag.reshape(o_ref.shape[1], o_ref.shape[3], n)


def cross(own, every, mates, groups):
    blocks, win, _, w, n = own.shape
    rounds = mates.shape[0]
    return pl.pallas_call(
        cross_kernel,
        grid_spec=pltpu.PrefetchScalarGridSpec(
            num_scalar_prefetch=1,
            grid=(blocks, rounds),
            in_specs=[
                pl.BlockSpec((1, win, 2, w, n), lambda b, r, m: (b, 0, 0, 0, 0)),
                pl.BlockSpec((1, win, 2, w, n), lambda b, r, m: (m[r, b], 0, 0, 0, 0)),
            ],
            out_specs=pl.BlockSpec(
                (1, groups, 1, n // groups, 2, n), lambda b, r, m: (b, 0, r, 0, 0, 0)
            ),
        ),
        out_shape=jax.ShapeDtypeStruct((blocks, groups, rounds, n // groups, 2, n), jnp.float32),
        compiler_params=pltpu.CompilerParams(vmem_limit_bytes=40 << 20),
        cost_estimate=pl.CostEstimate(
            flops=blocks * rounds * win * w * n * n * 8,
            bytes_accessed=blocks * (rounds + 1) * win * w * n * 4,
            transcendentals=0,
        ),
    )(mates, own, every)


def shards(spectra, partners):
    w, _, f, n = spectra.shape
    core = lax.axis_index("core")
    x = jnp.transpose(spectra, (2, 1, 0, 3))
    got = lax.all_to_all(x, ("zy", "win"), 0, 0, tiled=True)
    zy, win = 8, 8
    own = got.reshape(zy, win, 2, w, n)
    every = lax.all_gather(own, "core", axis=1, tiled=False).reshape(2 * zy, win, 2, w, n)
    mates = lax.dynamic_index_in_dim(
        partners.reshape(partners.shape[0], zy, 2), core, 2, keepdims=False
    )
    part = cross(own, every, mates, win)
    part = part.reshape((zy * win,) + part.shape[2:])
    back = lax.all_to_all(part, ("zy", "win"), 0, 0, tiled=True)
    return jnp.transpose(back, (1, 2, 3, 0, 4))[:, None]


def solution(mesh):
    split = Mesh(mesh.devices.reshape(8, 2, 8), ("zy", "core", "win"))
    return jax.shard_map(
        shards,
        mesh=split,
        in_specs=(P("win", None, None, ("zy", "core")), P()),
        out_specs=P(None, ("zy", "core"), "win", None, None, None),
        check_vma=False,
    )
```

time: 577 us -> 250 us (0.43)
  waiting for transfers between devices: 350 us -> 23 us
  blocking collectives: 0 us -> 152 us
  matrix products: 53.9 us -> 0 us
  local copies, waits for them, and re-layouts: 90.7 us -> 37.4 us
  other arithmetic: 42 us -> 0 us
  starting transfers between devices: 25.5 us -> 0.01 us
  Pallas kernels: 0 us -> 22.9 us
    reduce_scatter x3 -> x0, waiting for transfers between devices: 248 us -> none  [shards(): lax.psum_scatter(jnp.stack([real, imag], 2), 'win', scatter_dimension=0,...]
    all_to_all x0 -> x2, blocking collectives: none -> 152 us  [the longest x1 102 us: shards(): got = lax.all_to_all(x, ('zy', 'win'), 0, 0, tiled=True)]
    all_to_all x4 -> x0, waiting for transfers between devices: 103 us -> none  [the longest x1 88.9 us: shards(): lax.all_to_all(spectra[:, :, :, None, :], 'blk', split_axis=2, concat_axi...]
    dot_general x12 -> x0, matrix products: 53.9 us -> none  [the longest x3 17.4 us: complex_pair(): jnp.einsum(form, left[:, 1], right[:, 0], preferred_element_type=jnp.floa...]
    another operation x4 -> x1, local copies, waits for them, and re-layouts: 33.7 us -> 4.59 us  [shards(): lax.all_gather(own, 'core', axis=1, tiled=False)]
    another operation x4 -> x0, other arithmetic: 25.7 us -> none  [the longest x3 24.2 us: shards(): jnp.stack([real, imag], 2)]
    all_to_all x4 -> x0, starting transfers between devices: 24.9 us -> none  [the longest x3 17 us: shards(): lax.all_to_all(share, 'blk', split_axis=1, concat_axis=3, tiled=True)]
    gather x3 -> x0, local copies, waits for them, and re-layouts: 23.5 us -> none  [shards(): mates = jnp.take(spread, partners[step], axis=3)]
  transfers between devices with their start and end apart: 7 -> 1, of which waited for: 5 -> 1; matrix products, arithmetic and copies ran while one was open for 19% -> 3% of each run, Pallas kernels for 0% -> 0%
where the time goes in v1:
time: 250 us; the launch traced here: 249 us
  blocking collectives  152 us (61%)
  local copies, waits for them, and re-layouts  37.4 us (15%)
  waiting for transfers between devices  23 us (9%)
  Pallas kernels  22.9 us (9%)
  between operations  13.4 us (5%)
    all_to_all x1, blocking collectives, shards(): got = lax.all_to_all(x, ('zy', 'win'), 0, 0, tiled=True)  102 us
    all_to_all x1, blocking collectives, shards(): back = lax.all_to_all(part, ('zy', 'win'), 0, 0, tiled=True)  50 us
    all_gather x1, waiting for transfers between devices, shards(): lax.all_gather(own, 'core', axis=1, tiled=False)  23 us
    pallas_call x1, Pallas kernels, cross(): pl.pallas_call(cross_kernel, grid_spec=pltpu.PrefetchScalarGridSpec(num_s...  22.9 us
    unnamed x7, local copies, waits for them, and re-layouts  21.5 us
    all_to_all x1, local copies, waits for them, and re-layouts, shards(): got = lax.all_to_all(x, ('zy', 'win'), 0, 0, tiled=True)  7.5 us
  transfers between devices with their start and end apart: 1, of which 1 were waited for; matrix products, arithmetic and copies ran while one was open for 3% of the time, Pallas kernels for 0%

profile of v1, /device:TPU:1, one launch (start us, length us, event | category | flops | bytes accessed | tf_op | source)
XLA Modules:
  0.0 248.7 jit_solution(4936437419825456875)
XLA Ops:
  6.5 0.0 all-gather.2.cloned.1.call-start
  6.5 14.5 %copy.14 = bf16[240,2,64,128]{3,1,0,2:T(2,128)(2,1)S(1)} copy(bf16[240,2,64,128]{3,2,1,0:T(8,128)(2,1)} %param.2) | data formatting | bytes 15728640 | tf_op args[0]
  21.1 102.0 %all_to_all.10 = bf16[64,2,240,128]{3,1,2,0:T(2,128)(2,1)S(1)} all-to-all(bf16[64,2,240,128]{3,1,2,0:T(2,128)(2,1)S(1)} %bitcast.13), channel_id=1, replica_groups=mesh['zy'=8,'core'=2,'win'=8] {'zy','win'}, dimensions={0} | all-to-all | bytes 15728640 | tf_op jit(solution)/shard_map/all_to_all | solution.py:58
  123.0 0.0 copy-start.1
  123.0 3.1 %copy-done.1 = bf16[64,2,240,128]{3,1,2,0:T(2,128)(2,1)} copy-done((bf16[64,2,240,128]{3,1,2,0:T(2,128)(2,1)}, bf16[64,2,240,128]{3,1,2,0:T(2,128)(2,1)S(1)}, u32[]{:S(2)}) %copy-start.1) | copy-done | bytes 7864344
  126.1 4.6 %copy.11 = bf16[8,1,8,2,240,128]{5,4,3,2,1,0:T(8,128)(2,1)} copy(bf16[8,1,8,2,240,128]{5,3,4,2,0,1:T(2,128)(2,1)S(1)} %bitcast.12) | data formatting | bytes 15728640 | tf_op jit(solution)/shard_map/all_gather;reshape | solution.py:61
  130.7 0.0 copy-start.2
  130.7 0.0 all-gather.2.cloned.1.call-update
  130.8 0.7 copy-done.2
  131.4 0.1 reshape.12
  131.5 0.2 dynamic-slice_reduce_fusion.mates
  131.7 7.5 %copy.10 = bf16[64,2,240,128]{3,2,1,0:T(8,128)(2,1)} copy(bf16[64,2,240,128]{3,1,2,0:T(2,128)(2,1)} %copy-done.1) | data formatting | bytes 15728640 | tf_op jit(solution)/shard_map/all_to_all | solution.py:58
  139.2 23.0 %all-gather.2.cloned.1.call-done = bf16[8,2,8,2,240,128]{5,4,3,2,1,0:T(8,128)(2,1)} async-done(((bf16[8,1,8,2,240,128]{5,4,3,2,1,0:T(8,128)(2,1)}), bf16[8,2,8,2,240,128]{5,4,3,2,1,0:T(8,128)(2,1)}) %all-gather.2.cloned.1.call-update) | async-done | bytes 15728656 | tf_op jit(solution)/shard_map/all_gather | solution.py:61
  162.2 0.0 copy-start
  162.2 3.2 %copy-done = bf16[64,2,240,128]{3,2,1,0:T(8,128)(2,1)S(1)} copy-done((bf16[64,2,240,128]{3,2,1,0:T(8,128)(2,1)S(1)}, bf16[64,2,240,128]{3,2,1,0:T(8,128)(2,1)}, u32[]{:S(2)}) %copy-start) | copy-done | bytes 7864344
  165.4 22.9 %shard_map.28 = f32[8,8,3,16,2,128]{5,4,3,2,1,0:T(2,128)S(1)} custom-call(s32[3,8]{1,0:T(4,128)S(1)} %dynamic-slice_reduce_fusion.mates, bf16[8,8,2,240,128]{4,3,2,1,0:T(8,128)(2,1)S(1)} %bitcast.10, bf16[16,8,2,240,128]{4,3,2,1,0:T(8,128)(2,1)} %bitcast.14), custom_call_target="tpu_custom_call" | custom-call | flops 6039797760 | bytes 31457280 | tf_op jit(solution)/shard_map/pallas_call | solution.py:31
  188.3 50.0 %all_to_all.11 = f32[64,3,16,2,128]{4,3,2,1,0:T(2,128)S(1)} all-to-all(f32[64,3,16,2,128]{4,3,2,1,0:T(2,128)S(1)} %bitcast.11), channel_id=1, replica_groups=mesh['zy'=8,'core'=2,'win'=8] {'zy','win'}, dimensions={0} | all-to-all | bytes 6291456 | tf_op jit(solution)/shard_map/all_to_all | solution.py:67
  238.4 3.5 %copy.12 = f32[3,1,16,2,64,128]{5,4,3,2,1,0:T(8,128)} copy(f32[3,1,16,2,64,128]{5,3,2,0,4,1:T(2,128)S(1)} %bitcast.15) | data formatting | bytes 6291456 | tf_op jit(solution)/shard_map/broadcast_in_dim | solution.py:68
Async XLA Ops:
  6.5 155.7 %all-gather.2.cloned.1.call-start = ((), (), s32[]{:S(2)}) async-start(), calls=%async_computation.2 | async-start | bytes 23592960 | tf_op jit(solution)/shard_map/all_gather | solution.py:61
  123.0 3.1 %copy-start.1 = (bf16[64,2,240,128]{3,1,2,0:T(2,128)(2,1)}, bf16[64,2,240,128]{3,1,2,0:T(2,128)(2,1)S(1)}, u32[]{:S(2)}) copy-start(bf16[64,2,240,128]{3,1,2,0:T(2,128)(2,1)S(1)} %all_to_all.10) | copy-start | bytes 23592964
  130.7 0.7 copy-start.2
  162.2 3.2 %copy-start = (bf16[64,2,240,128]{3,2,1,0:T(8,128)(2,1)S(1)}, bf16[64,2,240,128]{3,2,1,0:T(8,128)(2,1)}, u32[]{:S(2)}) copy-start(bf16[64,2,240,128]{3,2,1,0:T(8,128)(2,1)} %copy.10) | copy-start | bytes 23592964
Sparse Core Ops, SparseCore 0:
  130.9 31.2 all-gather.1

commit v2 on v0

v2 whole, which is shorter than its diff:
```python
import functools

import jax
import jax.numpy as jnp
from jax import lax
from jax.experimental import pallas as pl
from jax.experimental.pallas import tpu as pltpu
from jax.sharding import PartitionSpec as P

MESH = pl.DeviceIdType.MESH
SIDE = 4
STEPS = (1, 3, 2)
ALL = slice(None)


def position():
    blk, win = lax.axis_index("blk"), lax.axis_index("win")
    return (win % 4, win // 4 * 2 + blk // 2 % 2, blk // 4), blk % 2


def device(place, core):
    x, y, z = place
    return (z * 4 + y % 2 * 2 + core, y // 2 * 4 + x)


def neighbour(place, core, axis, step):
    moved = list(place)
    moved[axis] = (moved[axis] + step) % SIDE
    return device(moved, core)


def pick(**chosen):
    return tuple(chosen.get(name, ALL) for name in "xyz")


class Exchange:
    def __init__(self, place, core, source, first, second, target, sems):
        self.place, self.core = place, core
        self.source, self.first, self.second, self.target = source, first, second, target
        self.sems = sems
        self.one, self.two, self.three, self.kept, self.sent = {}, {}, {}, {}, []

    def send(self, src, dst, which, at, axis, step):
        send_sem, recv_sem = self.sems[2 * which], self.sems[2 * which + 1]
        copy = pltpu.make_async_remote_copy(
            src_ref=src,
            dst_ref=dst,
            send_sem=send_sem.at[at],
            recv_sem=recv_sem.at[at],
            device_id=neighbour(self.place, self.core, axis, step),
            device_id_type=MESH,
        )
        copy.start()
        self.sent.append(copy)
        return copy

    def keep(self, src, dst, which, at):
        copy = pltpu.make_async_copy(src, dst, self.sems[2 * which + 1].at[at])
        copy.start()
        return copy

    def axes(self, t):
        return t, (t + 1) % 3, (t + 2) % 3

    def phase_one(self, t, d1):
        a1, _, _ = self.axes(t)
        there = (self.place[a1] + d1) % SIDE
        self.one[t, d1] = self.send(
            self.source(t, pick(**{"xyz"[a1]: there})),
            self.first.at[t, self.place[a1]],
            0,
            (t, d1),
            a1,
            d1,
        )

    def phase_two(self, t, d1):
        a1, a2, _ = self.axes(t)
        origin = (self.place[a1] - d1) % SIDE
        for d2 in STEPS + (0,):
            there = (self.place[a2] + d2) % SIDE
            if d1 == 0:
                src = self.source(t, pick(**{"xyz"[a1]: origin, "xyz"[a2]: there}))
            else:
                rest = [there if axis == a2 else ALL for axis in range(3) if axis != a1]
                src = self.first.at[(t, origin, *rest)]
            dst = self.second.at[t, self.place[a2], origin]
            at = (t, d1, d2)
            if d2 == 0:
                self.two[at] = self.keep(src, dst, 1, at)
            else:
                self.two[at] = self.send(src, dst, 1, at, a2, d2)

    def phase_three(self, t, d2):
        a1, a2, a3 = self.axes(t)
        origin = (self.place[a2] - d2) % SIDE
        for d1 in (0,) + STEPS:
            self.arrive(self.two[t, d1, d2], d2)
        for d3 in STEPS + (0,):
            there = (self.place[a3] + d3) % SIDE
            src = self.second.at[t, origin, :, there]
            dst = self.target(t, pick(**{"xyz"[a2]: origin, "xyz"[a3]: self.place[a3]}))
            at = (t, d2, d3)
            if d3 == 0:
                self.three[at] = self.keep(src, dst, 2, at)
            else:
                self.three[at] = self.send(src, dst, 2, at, a3, d3)

    def landed(self, t, d2, d3):
        _, a2, a3 = self.axes(t)
        return pick(
            **{
                "xyz"[a2]: (self.place[a2] - d2) % SIDE,
                "xyz"[a3]: (self.place[a3] - d3) % SIDE,
            }
        )

    def arrive(self, copy, step):
        if step == 0:
            copy.wait()
        else:
            copy.wait_recv()

    def finish(self):
        for copy in self.sent:
            copy.wait_send()


def kernel(
    mates, x_ref, o_ref, first, second, every, turned, part, first_out, second_out, *sems
):
    place, core = position()
    sibling = device(place, 1 - core)
    rounds = 3
    w = every.shape[-2]
    n = every.shape[-1]
    shift = x_ref.shape[-2] // 3

    barrier = pltpu.get_barrier_semaphore()
    for axis in range(3):
        for step in STEPS:
            pl.semaphore_signal(
                barrier,
                inc=1,
                device_id=neighbour(place, core, axis, step),
                device_id_type=MESH,
            )
    pl.semaphore_signal(barrier, inc=1, device_id=sibling, device_id_type=MESH)
    pl.semaphore_wait(barrier, 10)

    into = Exchange(
        place,
        core,
        lambda t, at: x_ref.at[(*at, ALL, pl.ds(t * shift, shift))],
        first,
        second,
        lambda t, at: every.at[(core, t, *at)],
        sems[0:6],
    )
    for d1 in STEPS:
        for t in range(3):
            into.phase_one(t, d1)
    for t in range(3):
        into.phase_two(t, 0)
    for d1 in STEPS:
        for t in range(3):
            into.arrive(into.one[t, d1], d1)
            into.phase_two(t, d1)
    for d2 in (0,) + STEPS:
        for t in range(3):
            into.phase_three(t, d2)
    swaps = []
    for d2 in (0,) + STEPS:
        for d3 in (0,) + STEPS:
            for t in range(3):
                into.arrive(into.three[t, d2, d3], d3)
                here = every.at[(core, t, *into.landed(t, d2, d3))]
                copy = pltpu.make_async_remote_copy(
                    src_ref=here,
                    dst_ref=here,
                    send_sem=sems[12].at[t, d2, d3],
                    recv_sem=sems[13].at[t, d2, d3],
                    device_id=sibling,
                    device_id_type=MESH,
                )
                copy.start()
                swaps.append(copy)
    for copy in swaps:
        copy.wait_recv()

    def wide(owner, y_lo, z):
        halves = []
        for q in range(2):
            rows = []
            for t in range(3):
                for y_hi in range(2):
                    for x in range(SIDE):
                        rows.append(every[owner, t, x, 2 * y_hi + y_lo, z, q])
            halves.append(jnp.concatenate(rows, axis=0))
        return jnp.concatenate(halves, axis=1)

    back = Exchange(
        place,
        core,
        lambda t, at: part.at[(t, *at)],
        first_out,
        second_out,
        lambda t, at: o_ref.at[(t, *at)],
        sems[6:12],
    )
    for r in range(rounds):

        @pl.loop(0, 2 * SIDE)
        def block(i):
            z, y_lo = i // 2, i % 2
            if r == 0:
                turned[i] = wide(core, y_lo, z).T
            mate = mates[r, i * 2 + core]
            g = jnp.dot(
                turned[i],
                wide(mate % 2, mate // 2 % 2, mate // 4),
                preferred_element_type=jnp.float32,
            )
            real = g[:n, :n] + g[n:, n:]
            imag = g[:n, n:] - g[n:, :n]
            rows = part.shape[-2]
            for y_hi in range(2):
                for x in range(SIDE):
                    cut = slice((y_hi * SIDE + x) * rows, (y_hi * SIDE + x + 1) * rows)
                    part[r, x, 2 * y_hi + y_lo, z, 0] = real[cut]
                    part[r, x, 2 * y_hi + y_lo, z, 1] = imag[cut]

        for d1 in STEPS:
            back.phase_one(r, d1)
        back.phase_two(r, 0)
    for d1 in STEPS:
        for t in range(3):
            back.arrive(back.one[t, d1], d1)
            back.phase_two(t, d1)
    for d2 in (0,) + STEPS:
        for t in range(3):
            back.phase_three(t, d2)
    for d2 in (0,) + STEPS:
        for d3 in (0,) + STEPS:
            for t in range(3):
                back.arrive(back.three[t, d2, d3], d3)
    into.finish()
    back.finish()
    for copy in swaps:
        copy.wait_send()


def cross(x, partners):
    _, _, _, _, windows, n = x.shape
    rows = n // 8
    third = windows // 3
    grid = (SIDE, SIDE)
    sems = pltpu.SemaphoreType.DMA
    exchange_sems = [sems((3, 4)), sems((3, 4))] + [sems((3, 4, 4))] * 4
    return pl.pallas_call(
        kernel,
        out_shape=jax.ShapeDtypeStruct((3, SIDE, SIDE, SIDE, 2, rows, n), jnp.float32),
        in_specs=[
            pl.BlockSpec(memory_space=pltpu.SMEM),
            pl.BlockSpec(memory_space=pl.ANY),
        ],
        out_specs=pl.BlockSpec(memory_space=pl.ANY),
        scratch_shapes=[
            pltpu.VMEM((3, SIDE, *grid, 2, third, n), jnp.bfloat16),
            pltpu.VMEM((3, SIDE, *grid, 2, third, n), jnp.bfloat16),
            pltpu.VMEM((2, 3, SIDE, *grid, 2, third, n), jnp.bfloat16),
            pltpu.VMEM((8, 2 * n, 8 * windows), jnp.bfloat16),
            pltpu.VMEM((3, SIDE, *grid, 2, rows, n), jnp.float32),
            pltpu.VMEM((3, SIDE, *grid, 2, rows, n), jnp.float32),
            pltpu.VMEM((3, SIDE, *grid, 2, rows, n), jnp.float32),
        ]
        + exchange_sems * 2
        + [sems((3, 4, 4))] * 2,
        compiler_params=pltpu.CompilerParams(
            collective_id=0, has_side_effects=True, vmem_limit_bytes=60 << 20
        ),
        cost_estimate=pl.CostEstimate(
            flops=24 * 8 * windows * n * n * 8,
            bytes_accessed=16 << 20,
            transcendentals=0,
        ),
        name="cross",
    )(partners, x)


def shards(spectra, partners):
    w, _, f, n = spectra.shape
    x = jnp.transpose(spectra, (2, 1, 0, 3)).reshape(SIDE, SIDE, SIDE, 2, w, n)
    back = cross(x, partners)
    back = back.reshape(3, f, 2, n // 8, n)
    return jnp.transpose(back, (0, 3, 2, 1, 4))[:, None]


def solution(mesh):
    return jax.shard_map(
        shards,
        mesh=mesh,
        in_specs=(P("win", None, None, "blk"), P()),
        out_specs=P(None, "blk", "win", None, None, None),
        check_vma=False,
    )
```

time: 577 us -> 163 us (0.28)
  waiting for transfers between devices: 350 us -> 0 us
  Pallas kernels: 0 us -> 146 us
  local copies, waits for them, and re-layouts: 90.7 us -> 16.7 us
  matrix products: 53.9 us -> 0 us
  other arithmetic: 42 us -> 0 us
  starting transfers between devices: 25.5 us -> 0 us
  between operations: 13.3 us -> 0.01 us
    reduce_scatter x3 -> x0, waiting for transfers between devices: 248 us -> none  [shards(): lax.psum_scatter(jnp.stack([real, imag], 2), 'win', scatter_dimension=0,...]
    pallas_call x0 -> x1, Pallas kernels: none -> 146 us  [cross(): pl.pallas_call(kernel, out_shape=jax.ShapeDtypeStruct((3, SIDE, SIDE, SID...]
    all_to_all x4 -> x0, waiting for transfers between devices: 103 us -> none  [the longest x1 88.9 us: shards(): lax.all_to_all(spectra[:, :, :, None, :], 'blk', split_axis=2, concat_axi...]
    dot_general x12 -> x0, matrix products: 53.9 us -> none  [the longest x3 17.4 us: complex_pair(): jnp.einsum(form, left[:, 1], right[:, 0], preferred_element_type=jnp.floa...]
    another operation x4 -> x0, local copies, waits for them, and re-layouts: 33.7 us -> none  [the longest x3 31.1 us: shards(): jnp.stack([real, imag], 2)]
    another operation x4 -> x0, other arithmetic: 25.7 us -> none  [the longest x3 24.2 us: shards(): jnp.stack([real, imag], 2)]
    all_to_all x4 -> x0, starting transfers between devices: 24.9 us -> none  [the longest x3 17 us: shards(): lax.all_to_all(share, 'blk', split_axis=1, concat_axis=3, tiled=True)]
    gather x3 -> x0, local copies, waits for them, and re-layouts: 23.5 us -> none  [shards(): mates = jnp.take(spread, partners[step], axis=3)]
  transfers between devices with their start and end apart: 7 -> 0, of which waited for: 5 -> 0; matrix products, arithmetic and copies ran while one was open for 19% -> 0% of each run, Pallas kernels for 0% -> 0%
where the time goes in v2:
time: 163 us
  Pallas kernels  146 us (90%)
  local copies, waits for them, and re-layouts  16.7 us (10%)
    pallas_call x1, Pallas kernels, cross(): pl.pallas_call(kernel, out_shape=jax.ShapeDtypeStruct((3, SIDE, SIDE, SID...  146 us
    transpose x1, local copies, waits for them, and re-layouts, shards(): x = jnp.transpose(spectra, (2, 1, 0, 3)).reshape(SIDE, SIDE, SIDE, 2, w, n)  11.4 us
    reshape x1, local copies, waits for them, and re-layouts, shards(): back = back.reshape(3, f, 2, n // 8, n)  5.38 us

profile of v2, /device:TPU:1, one launch (start us, length us, event | category | flops | bytes accessed | tf_op | source)
XLA Modules:
  0.0 163.2 jit_solution(10733729960148978524)
XLA Ops:
  0.0 11.4 %copy.3 = bf16[64,2,240,128]{3,2,1,0:T(8,128)(2,1)} copy(bf16[64,2,240,128]{3,0,1,2:T(8,128)(2,1)} %bitcast.8) | data formatting | bytes 15728640 | tf_op jit(solution)/shard_map/transpose | solution.py:293
  11.4 146.5 %cross.1 = f32[3,4,4,4,2,16,128]{6,5,4,3,2,1,0:T(8,128)} custom-call(s32[3,16]{1,0:T(4,128)} %mates.1, bf16[4,4,4,2,240,128]{5,4,3,2,1,0:T(8,128)(2,1)} %bitcast.9), custom_call_target="tpu_custom_call" | custom-call | flops 6039797760 | bytes 16777216 | tf_op jit(solution)/shard_map/cross/pallas_call | solution.py:260
  157.9 5.4 %copy.6 = f32[3,64,2,16,128]{4,1,2,3,0:T(8,128)} copy(f32[3,64,2,16,128]{4,3,2,1,0:T(8,128)} %bitcast.10) | data formatting | bytes 6291456 | tf_op jit(solution)/shard_map/reshape | solution.py:295

commit v3 on v2

--- a/solution.py
+++ b/solution.py
@@ -127,7 +127,20 @@
 
 
 def kernel(
-    mates, x_ref, o_ref, first, second, every, turned, part, first_out, second_out, *sems
+    mates,
+    spectra,
+    o_ref,
+    stage,
+    x_ref,
+    first,
+    second,
+    every,
+    turned,
+    part,
+    first_out,
+    second_out,
+    stage_sem,
+    *sems,
 ):
     place, core = position()
     sibling = device(place, 1 - core)
@@ -135,6 +148,18 @@
     w = every.shape[-2]
     n = every.shape[-1]
     shift = x_ref.shape[-2] // 3
+    slots, cut_rows = stage.shape[:2]
+    pieces = x_ref.shape[-2] // cut_rows
+
+    def load(i):
+        return pltpu.make_async_copy(
+            spectra.at[pl.ds(i * cut_rows, cut_rows)],
+            stage.at[i % slots],
+            stage_sem.at[i % slots],
+        )
+
+    for i in range(slots):
+        load(i).start()
 
     barrier = pltpu.get_barrier_semaphore()
     for axis in range(3):
@@ -146,6 +171,24 @@
                 device_id_type=MESH,
             )
     pl.semaphore_signal(barrier, inc=1, device_id=sibling, device_id_type=MESH)
+
+    def relayout(t):
+        @pl.loop(t * pieces // 3, (t + 1) * pieces // 3)
+        def piece(i):
+            load(i).wait()
+            rows = pl.ds(pl.multiple_of(i * cut_rows, cut_rows), cut_rows)
+            for q in range(2):
+                for x in range(SIDE):
+                    v = stage[i % slots, :, q, x * 16 : (x + 1) * 16, :]
+                    v = jnp.swapaxes(v, 0, 1).reshape(SIDE, SIDE, cut_rows, n)
+                    x_ref[x, :, :, q, rows, :] = v
+
+            @pl.when(i + slots < pieces)
+            def _():
+                load(i + slots).start()
+
+    relayout(0)
+    relayout(1)
     pl.semaphore_wait(barrier, 10)
 
     into = Exchange(
@@ -158,8 +201,11 @@
         sems[0:6],
     )
     for d1 in STEPS:
-        for t in range(3):
+        for t in range(2):
             into.phase_one(t, d1)
+    relayout(2)
+    for d1 in STEPS:
+        into.phase_one(2, d1)
     for t in range(3):
         into.phase_two(t, 0)
     for d1 in STEPS:
@@ -251,7 +297,7 @@
 
 
 def cross(x, partners):
-    _, _, _, _, windows, n = x.shape
+    windows, _, _, n = x.shape
     rows = n // 8
     third = windows // 3
     grid = (SIDE, SIDE)
@@ -266,6 +312,8 @@
         ],
         out_specs=pl.BlockSpec(memory_space=pl.ANY),
         scratch_shapes=[
+            pltpu.VMEM((4, 16, 2, SIDE**3, n), jnp.bfloat16),
+            pltpu.VMEM((SIDE, *grid, 2, windows, n), jnp.bfloat16),
             pltpu.VMEM((3, SIDE, *grid, 2, third, n), jnp.bfloat16),
             pltpu.VMEM((3, SIDE, *grid, 2, third, n), jnp.bfloat16),
             pltpu.VMEM((2, 3, SIDE, *grid, 2, third, n), jnp.bfloat16),
@@ -274,6 +322,7 @@
             pltpu.VMEM((3, SIDE, *grid, 2, rows, n), jnp.float32),
             pltpu.VMEM((3, SIDE, *grid, 2, rows, n), jnp.float32),
         ]
+        + [sems((4,))]
         + exchange_sems * 2
         + [sems((3, 4, 4))] * 2,
         compiler_params=pltpu.CompilerParams(
@@ -290,8 +339,7 @@
 
 def shards(spectra, partners):
     w, _, f, n = spectra.shape
-    x = jnp.transpose(spectra, (2, 1, 0, 3)).reshape(SIDE, SIDE, SIDE, 2, w, n)
-    back = cross(x, partners)
+    back = cross(spectra, partners)
     back = back.reshape(3, f, 2, n // 8, n)
     return jnp.transpose(back, (0, 3, 2, 1, 4))[:, None]
 

time: 163 us -> 156 us (0.957)
  local copies, waits for them, and re-layouts: 16.7 us -> 5.38 us
  Pallas kernels: 146 us -> 150 us
    transpose x1 -> x0, local copies, waits for them, and re-layouts: 11.4 us -> none  [shards(): x = jnp.transpose(spectra, (2, 1, 0, 3)).reshape(SIDE, SIDE, SIDE, 2, w, n)]
    pallas_call x1, Pallas kernels: 146 us -> 150 us  [cross(): pl.pallas_call(kernel, out_shape=jax.ShapeDtypeStruct((3, SIDE, SIDE, SID...]
where the time goes in v3:
time: 156 us; the launch traced here: 155 us
  Pallas kernels  150 us (96%)
  local copies, waits for them, and re-layouts  5.38 us (3%)
    pallas_call x1, Pallas kernels, cross(): pl.pallas_call(kernel, out_shape=jax.ShapeDtypeStruct((3, SIDE, SIDE, SID...  150 us
    reshape x1, local copies, waits for them, and re-layouts, shards(): back = back.reshape(3, f, 2, n // 8, n)  5.38 us

profile of v3, /device:TPU:1, one launch (start us, length us, event | category | flops | bytes accessed | tf_op | source)
XLA Modules:
  0.0 155.1 jit_solution(11269471741701417836)
XLA Ops:
  0.0 149.7 %cross.1 = f32[3,4,4,4,2,16,128]{6,5,4,3,2,1,0:T(8,128)} custom-call(s32[3,16]{1,0:T(4,128)} %mates.1, bf16[240,2,64,128]{3,2,1,0:T(8,128)(2,1)} %spectra.1), custom_call_target="tpu_custom_call" | custom-call | flops 6039797760 | bytes 16777216 | tf_op jit(solution)/shard_map/cross/pallas_call | solution.py:306
  149.7 5.4 %copy.5 = f32[3,64,2,16,128]{4,1,2,3,0:T(8,128)} copy(f32[3,64,2,16,128]{4,3,2,1,0:T(8,128)} %bitcast.6) | data formatting | bytes 6291456 | tf_op jit(solution)/shard_map/reshape | solution.py:343

commit v4 on v3

--- a/solution.py
+++ b/solution.py
@@ -11,6 +11,8 @@
 SIDE = 4
 STEPS = (1, 3, 2)
 ALL = slice(None)
+CODES = 32767.0
+TINY = 1e-36
 
 
 def position():
@@ -31,6 +33,12 @@
 
 def pick(**chosen):
     return tuple(chosen.get(name, ALL) for name in "xyz")
+
+
+def encode(value, scale):
+    root = jnp.sqrt(jnp.sqrt(jnp.abs(value) * scale))
+    code = (root * CODES + 0.5).astype(jnp.int32)
+    return jnp.where(value < 0, -code, code).astype(jnp.int16)
 
 
 class Exchange:
@@ -130,16 +138,22 @@
     mates,
     spectra,
     o_ref,
+    scales,
     stage,
     x_ref,
     first,
     second,
     every,
     turned,
+    product,
+    largest,
     part,
     first_out,
     second_out,
     stage_sem,
+    scale_keep,
+    scale_send,
+    scale_recv,
     *sems,
 ):
     place, core = position()
@@ -255,6 +269,7 @@
         sems[6:12],
     )
     for r in range(rounds):
+        largest[r] = jnp.zeros_like(largest[r])
 
         @pl.loop(0, 2 * SIDE)
         def block(i):
@@ -269,31 +284,103 @@
             )
             real = g[:n, :n] + g[n:, n:]
             imag = g[:n, n:] - g[n:, :n]
+            both = jnp.maximum(jnp.abs(real), jnp.abs(imag)).reshape(-1, 8, n)
+            largest[r] = jnp.maximum(largest[r], jnp.max(both, axis=0))
             rows = part.shape[-2]
             for y_hi in range(2):
                 for x in range(SIDE):
                     cut = slice((y_hi * SIDE + x) * rows, (y_hi * SIDE + x + 1) * rows)
-                    part[r, x, 2 * y_hi + y_lo, z, 0] = real[cut]
-                    part[r, x, 2 * y_hi + y_lo, z, 1] = imag[cut]
+                    product[x, 2 * y_hi + y_lo, z, 0] = real[cut]
+                    product[x, 2 * y_hi + y_lo, z, 1] = imag[cut]
+
+        top = jnp.maximum(jnp.max(largest[r], keepdims=True), TINY)
+        largest[r] = jnp.broadcast_to(top, largest.shape[1:])
+        scale = 1.0 / jnp.broadcast_to(top, (1, n))
+
+        @pl.loop(0, SIDE * SIDE)
+        def code(i):
+            for z in range(SIDE):
+                for q in range(2):
+                    part[r, i // SIDE, i % SIDE, z, q] = encode(
+                        product[i // SIDE, i % SIDE, z, q], scale
+                    )
 
         for d1 in STEPS:
             back.phase_one(r, d1)
         back.phase_two(r, 0)
+
+    def scale_send_along(axis):
+        at = tuple(ALL if other < axis else place[other] for other in range(3))
+        here = scales.at[(ALL, *at)]
+        copies = []
+        for step in STEPS:
+            copy = pltpu.make_async_remote_copy(
+                src_ref=here,
+                dst_ref=here,
+                send_sem=scale_send.at[axis, step],
+                recv_sem=scale_recv.at[axis, step],
+                device_id=neighbour(place, core, axis, step),
+                device_id_type=MESH,
+            )
+            copy.start()
+            copies.append(copy)
+        return copies
+
+    kept = pltpu.make_async_copy(
+        largest.at[:, pl.ds(0, 1)], scales.at[(ALL, *place)], scale_keep
+    )
+    kept.start()
+    kept.wait()
+    shared = scale_send_along(0)
     for d1 in STEPS:
         for t in range(3):
             back.arrive(back.one[t, d1], d1)
             back.phase_two(t, d1)
+    for copy in shared[:3]:
+        copy.wait_recv()
+    shared += scale_send_along(1)
     for d2 in (0,) + STEPS:
         for t in range(3):
             back.phase_three(t, d2)
+    for copy in shared[3:6]:
+        copy.wait_recv()
+    shared += scale_send_along(2)
     for d2 in (0,) + STEPS:
         for d3 in (0,) + STEPS:
             for t in range(3):
                 back.arrive(back.three[t, d2, d3], d3)
+    for copy in shared[6:]:
+        copy.wait_recv()
+    for copy in shared:
+        copy.wait_send()
     into.finish()
     back.finish()
     for copy in swaps:
         copy.wait_send()
+
+
+def decode_kernel(codes, scales, o_ref):
+    n = codes.shape[-1]
+    share = codes[0, :, 0].astype(jnp.int32).astype(jnp.float32) * (1.0 / CODES)
+    value = share * share * (share * jnp.abs(share))
+    value = jnp.swapaxes(value, 0, 1)
+    o_ref[0, 0, :, 0] = value * scales[0].reshape(1, -1, n)
+
+
+def decode(codes, scales):
+    rounds, f, _, rows, n = codes.shape
+    return pl.pallas_call(
+        decode_kernel,
+        grid=(rounds, 2),
+        out_shape=jax.ShapeDtypeStruct((rounds, 1, rows, 2, f, n), jnp.float32),
+        in_specs=[
+            pl.BlockSpec((1, f, 1, rows, n), lambda r, q: (r, 0, q, 0, 0)),
+            pl.BlockSpec((1, f, 1, n), lambda r, q: (r, 0, 0, 0)),
+        ],
+        out_specs=pl.BlockSpec((1, 1, rows, 1, f, n), lambda r, q: (r, 0, 0, q, 0, 0)),
+        compiler_params=pltpu.CompilerParams(vmem_limit_bytes=16 << 20),
+        name="decode",
+    )(codes, scales)
 
 
 def cross(x, partners):
@@ -305,12 +392,15 @@
     exchange_sems = [sems((3, 4)), sems((3, 4))] + [sems((3, 4, 4))] * 4
     return pl.pallas_call(
         kernel,
-        out_shape=jax.ShapeDtypeStruct((3, SIDE, SIDE, SIDE, 2, rows, n), jnp.float32),
+        out_shape=[
+            jax.ShapeDtypeStruct((3, SIDE, *grid, 2, rows, n), jnp.int16),
+            jax.ShapeDtypeStruct((3, SIDE, *grid, 1, n), jnp.float32),
+        ],
         in_specs=[
             pl.BlockSpec(memory_space=pltpu.SMEM),
             pl.BlockSpec(memory_space=pl.ANY),
         ],
-        out_specs=pl.BlockSpec(memory_space=pl.ANY),
+        out_specs=[pl.BlockSpec(memory_space=pl.ANY)] * 2,
         scratch_shapes=[
             pltpu.VMEM((4, 16, 2, SIDE**3, n), jnp.bfloat16),
             pltpu.VMEM((SIDE, *grid, 2, windows, n), jnp.bfloat16),
@@ -318,11 +408,13 @@
             pltpu.VMEM((3, SIDE, *grid, 2, third, n), jnp.bfloat16),
             pltpu.VMEM((2, 3, SIDE, *grid, 2, third, n), jnp.bfloat16),
             pltpu.VMEM((8, 2 * n, 8 * windows), jnp.bfloat16),
-            pltpu.VMEM((3, SIDE, *grid, 2, rows, n), jnp.float32),
-            pltpu.VMEM((3, SIDE, *grid, 2, rows, n), jnp.float32),
-            pltpu.VMEM((3, SIDE, *grid, 2, rows, n), jnp.float32),
+            pltpu.VMEM((SIDE, *grid, 2, rows, n), jnp.float32),
+            pltpu.VMEM((3, 8, n), jnp.float32),
+            pltpu.VMEM((3, SIDE, *grid, 2, rows, n), jnp.int16),
+            pltpu.VMEM((3, SIDE, *grid, 2, rows, n), jnp.int16),
+            pltpu.VMEM((3, SIDE, *grid, 2, rows, n), jnp.int16),
         ]
-        + [sems((4,))]
+        + [sems((4,)), sems, sems((3, 4)), sems((3, 4))]
         + exchange_sems * 2
         + [sems((3, 4, 4))] * 2,
         compiler_params=pltpu.CompilerParams(
@@ -339,9 +431,8 @@
 
 def shards(spectra, partners):
     w, _, f, n = spectra.shape
-    back = cross(spectra, partners)
-    back = back.reshape(3, f, 2, n // 8, n)
-    return jnp.transpose(back, (0, 3, 2, 1, 4))[:, None]
+    codes, scales = cross(spectra, partners)
+    return decode(codes.reshape(3, f, 2, n // 8, n), scales.reshape(3, f, 1, n))
 
 
 def solution(mesh):

time: 156 us -> 147 us (0.942)
  Pallas kernels: 150 us -> 144 us
  local copies, waits for them, and re-layouts: 5.38 us -> 2.29 us
    pallas_call x1 -> x2, Pallas kernels: 150 us -> 144 us  [the longest x1 141 us: cross(): pl.pallas_call(kernel, out_shape=[jax.ShapeDtypeStruct((3, SIDE, *grid, 2...]
    reshape x1 -> x0, local copies, waits for them, and re-layouts: 5.38 us -> none  [shards(): back = back.reshape(3, f, 2, n // 8, n)]
    unnamed x0 -> x4, local copies, waits for them, and re-layouts: none -> 2.29 us
where the time goes in v4:
time: 147 us; the launch traced here: 146 us
  Pallas kernels  144 us (98%)
  local copies, waits for them, and re-layouts  2.29 us (2%)
    pallas_call x1, Pallas kernels, cross(): pl.pallas_call(kernel, out_shape=[jax.ShapeDtypeStruct((3, SIDE, *grid, 2...  141 us
    pallas_call x1, Pallas kernels, decode(): pl.pallas_call(decode_kernel, grid=(rounds, 2), out_shape=jax.ShapeDtypeS...  3.48 us

profile of v4, /device:TPU:1, one launch (start us, length us, event | category | flops | bytes accessed | tf_op | source)
XLA Modules:
  0.0 146.5 jit_solution(567982165533156486)
XLA Ops:
  0.0 140.7 %cross.1 = (s16[3,4,4,4,2,16,128]{6,5,4,3,2,1,0:T(8,128)(2,1)}, f32[3,4,4,4,1,128]{5,4,3,2,1,0:T(1,128)}) custom-call(s32[3,16]{1,0:T(4,128)} %mates.1, bf16[240,2,64,128]{3,2,1,0:T(8,128)(2,1)} %spectra.1), custom_call_target="tpu_custom_call" | custom-call | flops 6039797760 | bytes 16777216 | tf_op jit(solution)/shard_map/cross/pallas_call | solution.py:393
  140.7 0.0 copy-start
  140.7 1.4 copy-done
  142.1 0.0 copy-start.1
  142.1 0.9 copy-done.1
  143.0 3.5 %decode.1 = f32[3,1,16,2,64,128]{5,4,3,2,1,0:T(8,128)} custom-call(s16[3,64,2,16,128]{4,3,2,1,0:T(8,128)(2,1)S(1)} %bitcast.2, f32[3,64,1,128]{3,2,1,0:T(1,128)S(1)} %bitcast.3), custom_call_target="tpu_custom_call" | custom-call | tf_op jit(solution)/shard_map/decode/pallas_call | solution.py:372
Async XLA Ops:
  140.7 1.4 copy-start
  142.1 0.9 copy-start.1

commit v5 on v4

--- a/solution.py
+++ b/solution.py
@@ -11,6 +11,7 @@
 SIDE = 4
 STEPS = (1, 3, 2)
 ALL = slice(None)
+SHARES = (48, 32)
 CODES = 32767.0
 TINY = 1e-36
 
@@ -36,7 +37,9 @@
 
 
 def encode(value, scale):
-    root = jnp.sqrt(jnp.sqrt(jnp.abs(value) * scale))
+    share = jnp.abs(value) * scale + 1e-20
+    root = share * lax.rsqrt(share)
+    root = root * lax.rsqrt(root)
     code = (root * CODES + 0.5).astype(jnp.int32)
     return jnp.where(value < 0, -code, code).astype(jnp.int16)
 
@@ -134,46 +137,41 @@
             copy.wait_send()
 
 
-def kernel(
-    mates,
-    spectra,
-    o_ref,
-    scales,
-    stage,
-    x_ref,
-    first,
-    second,
-    every,
-    turned,
-    product,
-    largest,
-    part,
-    first_out,
-    second_out,
-    stage_sem,
-    scale_keep,
-    scale_send,
-    scale_recv,
-    *sems,
-):
+def kernel(mates, spectra, o_ref, scales, *scratch):
+    scratch = list(scratch)
+
+    def take(count):
+        taken = scratch[:count]
+        del scratch[:count]
+        return taken
+
+    (stage,) = take(1)
+    shares = len(SHARES)
+    ready, first, second, every = take(shares), take(shares), take(shares), take(shares)
+    turned, product, largest, part, first_out, second_out = take(6)
+    stage_sem, scale_keep, scale_send, scale_recv = take(4)
+    swap_send, swap_recv = take(shares), take(shares)
     place, core = position()
     sibling = device(place, 1 - core)
-    rounds = 3
-    w = every.shape[-2]
-    n = every.shape[-1]
-    shift = x_ref.shape[-2] // 3
+    rounds, n = product.shape[0], product.shape[-1]
     slots, cut_rows = stage.shape[:2]
-    pieces = x_ref.shape[-2] // cut_rows
-
-    def load(i):
+    third = sum(SHARES)
+    order = [
+        (h, t, t * third + sum(SHARES[:h]) + k * cut_rows, k * cut_rows)
+        for h in range(shares)
+        for t in range(3)
+        for k in range(SHARES[h] // cut_rows)
+    ]
+
+    def load(j):
         return pltpu.make_async_copy(
-            spectra.at[pl.ds(i * cut_rows, cut_rows)],
-            stage.at[i % slots],
-            stage_sem.at[i % slots],
-        )
-
-    for i in range(slots):
-        load(i).start()
+            spectra.at[pl.ds(order[j][2], cut_rows)],
+            stage.at[j % slots],
+            stage_sem.at[j % slots],
+        )
+
+    for j in range(slots):
+        load(j).start()
 
     barrier = pltpu.get_barrier_semaphore()
     for axis in range(3):
@@ -186,79 +184,34 @@
             )
     pl.semaphore_signal(barrier, inc=1, device_id=sibling, device_id_type=MESH)
 
-    def relayout(t):
-        @pl.loop(t * pieces // 3, (t + 1) * pieces // 3)
-        def piece(i):
-            load(i).wait()
-            rows = pl.ds(pl.multiple_of(i * cut_rows, cut_rows), cut_rows)
-            for q in range(2):
-                for x in range(SIDE):
-                    v = stage[i % slots, :, q, x * 16 : (x + 1) * 16, :]
-                    v = jnp.swapaxes(v, 0, 1).reshape(SIDE, SIDE, cut_rows, n)
-                    x_ref[x, :, :, q, rows, :] = v
-
-            @pl.when(i + slots < pieces)
-            def _():
-                load(i + slots).start()
-
-    relayout(0)
-    relayout(1)
-    pl.semaphore_wait(barrier, 10)
-
-    into = Exchange(
-        place,
-        core,
-        lambda t, at: x_ref.at[(*at, ALL, pl.ds(t * shift, shift))],
-        first,
-        second,
-        lambda t, at: every.at[(core, t, *at)],
-        sems[0:6],
-    )
-    for d1 in STEPS:
-        for t in range(2):
-            into.phase_one(t, d1)
-    relayout(2)
-    for d1 in STEPS:
-        into.phase_one(2, d1)
-    for t in range(3):
-        into.phase_two(t, 0)
-    for d1 in STEPS:
-        for t in range(3):
-            into.arrive(into.one[t, d1], d1)
-            into.phase_two(t, d1)
-    for d2 in (0,) + STEPS:
-        for t in range(3):
-            into.phase_three(t, d2)
-    swaps = []
-    for d2 in (0,) + STEPS:
-        for d3 in (0,) + STEPS:
-            for t in range(3):
-                into.arrive(into.three[t, d2, d3], d3)
-                here = every.at[(core, t, *into.landed(t, d2, d3))]
-                copy = pltpu.make_async_remote_copy(
-                    src_ref=here,
-                    dst_ref=here,
-                    send_sem=sems[12].at[t, d2, d3],
-                    recv_sem=sems[13].at[t, d2, d3],
-                    device_id=sibling,
-                    device_id_type=MESH,
-                )
-                copy.start()
-                swaps.append(copy)
-    for copy in swaps:
-        copy.wait_recv()
-
-    def wide(owner, y_lo, z):
-        halves = []
-        for q in range(2):
-            rows = []
-            for t in range(3):
-                for y_hi in range(2):
-                    for x in range(SIDE):
-                        rows.append(every[owner, t, x, 2 * y_hi + y_lo, z, q])
-            halves.append(jnp.concatenate(rows, axis=0))
-        return jnp.concatenate(halves, axis=1)
-
+    def relayout(share, thirds):
+        for j, (h, t, _, row) in enumerate(order):
+            if h != share or t not in thirds:
+                continue
+            load(j).wait()
+
+            @pl.loop(0, 2 * SIDE)
+            def turn(i):
+                q, x = i // SIDE, i % SIDE
+                v = stage[j % slots, :, q, pl.ds(pl.multiple_of(x * 16, 16), 16), :]
+                v = jnp.swapaxes(v, 0, 1).reshape(SIDE, SIDE, cut_rows, n)
+                ready[h][t, x, :, :, q, row : row + cut_rows, :] = v
+
+            if j + slots < len(order):
+                load(j + slots).start()
+
+    into = [
+        Exchange(
+            place,
+            core,
+            lambda t, at, h=h: ready[h].at[(t, *at)],
+            first[h],
+            second[h],
+            lambda t, at, h=h: every[h].at[(core, t, *at)],
+            take(6),
+        )
+        for h in range(shares)
+    ]
     back = Exchange(
         place,
         core,
@@ -266,48 +219,138 @@
         first_out,
         second_out,
         lambda t, at: o_ref.at[(t, *at)],
-        sems[6:12],
+        take(6),
     )
-    for r in range(rounds):
-        largest[r] = jnp.zeros_like(largest[r])
-
-        @pl.loop(0, 2 * SIDE)
-        def block(i):
-            z, y_lo = i // 2, i % 2
-            if r == 0:
-                turned[i] = wide(core, y_lo, z).T
-            mate = mates[r, i * 2 + core]
-            g = jnp.dot(
-                turned[i],
-                wide(mate % 2, mate // 2 % 2, mate // 4),
-                preferred_element_type=jnp.float32,
-            )
-            real = g[:n, :n] + g[n:, n:]
-            imag = g[:n, n:] - g[n:, :n]
-            both = jnp.maximum(jnp.abs(real), jnp.abs(imag)).reshape(-1, 8, n)
-            largest[r] = jnp.maximum(largest[r], jnp.max(both, axis=0))
-            rows = part.shape[-2]
-            for y_hi in range(2):
-                for x in range(SIDE):
-                    cut = slice((y_hi * SIDE + x) * rows, (y_hi * SIDE + x + 1) * rows)
-                    product[x, 2 * y_hi + y_lo, z, 0] = real[cut]
-                    product[x, 2 * y_hi + y_lo, z, 1] = imag[cut]
-
-        top = jnp.maximum(jnp.max(largest[r], keepdims=True), TINY)
+    swaps = []
+
+    def swap(h, d2):
+        for d3 in (0,) + STEPS:
+            for t in range(3):
+                into[h].arrive(into[h].three[t, d2, d3], d3)
+                here = every[h].at[(core, t, *into[h].landed(t, d2, d3))]
+                copy = pltpu.make_async_remote_copy(
+                    src_ref=here,
+                    dst_ref=here,
+                    send_sem=swap_send[h].at[t, d2, d3],
+                    recv_sem=swap_recv[h].at[t, d2, d3],
+                    device_id=sibling,
+                    device_id_type=MESH,
+                )
+                copy.start()
+                swaps.append((h, copy))
+
+    def swapped(h):
+        for share, copy in swaps:
+            if share == h:
+                copy.wait_recv()
+
+    def wide(h, owner, y_lo, z):
+        halves = []
+        for q in range(2):
+            rows = []
+            for t in range(3):
+                for y_hi in range(2):
+                    for x in range(SIDE):
+                        rows.append(every[h][owner, t, x, 2 * y_hi + y_lo, z, q])
+            halves.append(jnp.concatenate(rows, axis=0))
+        return jnp.concatenate(halves, axis=1)
+
+    def multiply(h, r, i):
+        depth = 24 * SHARES[h]
+        z, y_lo = i // 2, i % 2
+        if r == 0:
+            turned[i, :, :depth] = wide(h, core, y_lo, z).T
+        mate = mates[r, i * 2 + core]
+        g = jnp.dot(
+            turned[i, :, :depth],
+            wide(h, mate % 2, mate // 2 % 2, mate // 4),
+            preferred_element_type=jnp.float32,
+        )
+        sums = (g[:n, :n] + g[n:, n:], g[:n, n:] - g[n:, :n])
+        rows = product.shape[-2]
+        at = lambda k: (r, k % SIDE, k // SIDE * 2 + y_lo, z)
+        if h:
+            old = [
+                jnp.concatenate([product[(*at(k), q)] for k in range(2 * SIDE)], axis=0)
+                for q in range(2)
+            ]
+            sums = (sums[0] + old[0], sums[1] + old[1])
+        for k in range(2 * SIDE):
+            for q in range(2):
+                product[(*at(k), q)] = sums[q][k * rows : (k + 1) * rows]
+        return jnp.maximum(jnp.abs(sums[0]), jnp.abs(sums[1])).reshape(-1, 8, n)
+
+    def products(h, r):
+        @pl.loop(0, 2)
+        def blocks(j):
+            for k in range(SIDE):
+                multiply(h, r, j * SIDE + k)
+
+    def code(r, i, scale):
+        for z in range(SIDE):
+            for q in range(2):
+                part[r, i // SIDE, i % SIDE, z, q] = encode(
+                    product[r, i // SIDE, i % SIDE, z, q], scale
+                )
+
+    def scale_of(r, top):
+        top = jnp.maximum(jnp.max(jnp.max(top, axis=0), keepdims=True), TINY)
         largest[r] = jnp.broadcast_to(top, largest.shape[1:])
-        scale = 1.0 / jnp.broadcast_to(top, (1, n))
-
-        @pl.loop(0, SIDE * SIDE)
-        def code(i):
-            for z in range(SIDE):
-                for q in range(2):
-                    part[r, i // SIDE, i % SIDE, z, q] = encode(
-                        product[i // SIDE, i % SIDE, z, q], scale
-                    )
-
+        return 1.0 / jnp.broadcast_to(top, (1, n))
+
+    for h in range(shares):
+        for thirds in ((0, 1), (2,)) if h == 0 else ((0, 1, 2),):
+            relayout(h, thirds)
+            if h == 0 and thirds[0] == 0:
+                pl.semaphore_wait(barrier, 10)
+            for d1 in STEPS:
+                for t in thirds:
+                    into[h].phase_one(t, d1)
+        for t in range(3):
+            into[h].phase_two(t, 0)
+    for h in range(shares):
         for d1 in STEPS:
-            back.phase_one(r, d1)
-        back.phase_two(r, 0)
+            for t in range(3):
+                into[h].arrive(into[h].one[t, d1], d1)
+                into[h].phase_two(t, d1)
+    for h in range(shares):
+        if h >= 2:
+            for d2 in (0,) + STEPS:
+                swap(h - 2, d2)
+            swapped(h - 2)
+            for r in range(rounds):
+                products(h - 2, r)
+        for d2 in (0,) + STEPS:
+            for t in range(3):
+                into[h].phase_three(t, d2)
+    last = shares - 1
+    for d2 in (0,) + STEPS:
+        swap(last - 1, d2)
+    swapped(last - 1)
+    products(last - 1, 0)
+    swap(last, 0)
+    products(last - 1, 1)
+    swap(last, STEPS[0])
+    products(last - 1, 2)
+    swap(last, STEPS[1])
+    swap(last, STEPS[2])
+    swapped(shares - 1)
+
+    scale = None
+    for r in range(rounds + 1):
+        tops = []
+        for i in range(2 * SIDE):
+            if r < rounds:
+                tops.append(jnp.max(multiply(last, r, i), axis=0))
+            if r:
+                code(r - 1, 2 * i, scale)
+                code(r - 1, 2 * i + 1, scale)
+        if r < rounds:
+            scale = scale_of(r, jnp.stack(tops))
+        if r:
+            for d1 in STEPS:
+                back.phase_one(r - 1, d1)
+            back.phase_two(r - 1, 0)
 
     def scale_send_along(axis):
         at = tuple(ALL if other < axis else place[other] for other in range(3))
@@ -353,9 +396,10 @@
         copy.wait_recv()
     for copy in shared:
         copy.wait_send()
-    into.finish()
+    for exchange in into:
+        exchange.finish()
     back.finish()
-    for copy in swaps:
+    for _, copy in swaps:
         copy.wait_send()
 
 
@@ -378,7 +422,7 @@
             pl.BlockSpec((1, f, 1, n), lambda r, q: (r, 0, 0, 0)),
         ],
         out_specs=pl.BlockSpec((1, 1, rows, 1, f, n), lambda r, q: (r, 0, 0, q, 0, 0)),
-        compiler_params=pltpu.CompilerParams(vmem_limit_bytes=16 << 20),
+        compiler_params=pltpu.CompilerParams(vmem_limit_bytes=60 << 20),
         name="decode",
     )(codes, scales)
 
@@ -386,7 +430,6 @@
 def cross(x, partners):
     windows, _, _, n = x.shape
     rows = n // 8
-    third = windows // 3
     grid = (SIDE, SIDE)
     sems = pltpu.SemaphoreType.DMA
     exchange_sems = [sems((3, 4)), sems((3, 4))] + [sems((3, 4, 4))] * 4
@@ -401,22 +444,18 @@
             pl.BlockSpec(memory_space=pl.ANY),
         ],
         out_specs=[pl.BlockSpec(memory_space=pl.ANY)] * 2,
-        scratch_shapes=[
-            pltpu.VMEM((4, 16, 2, SIDE**3, n), jnp.bfloat16),
-            pltpu.VMEM((SIDE, *grid, 2, windows, n), jnp.bfloat16),
-            pltpu.VMEM((3, SIDE, *grid, 2, third, n), jnp.bfloat16),
-            pltpu.VMEM((3, SIDE, *grid, 2, third, n), jnp.bfloat16),
-            pltpu.VMEM((2, 3, SIDE, *grid, 2, third, n), jnp.bfloat16),
-            pltpu.VMEM((8, 2 * n, 8 * windows), jnp.bfloat16),
-            pltpu.VMEM((SIDE, *grid, 2, rows, n), jnp.float32),
+        scratch_shapes=[pltpu.VMEM((4, 16, 2, SIDE**3, n), jnp.bfloat16)]
+        + [pltpu.VMEM((3, SIDE, *grid, 2, share, n), jnp.bfloat16) for share in SHARES] * 3
+        + [pltpu.VMEM((2, 3, SIDE, *grid, 2, share, n), jnp.bfloat16) for share in SHARES]
+        + [
+            pltpu.VMEM((8, 2 * n, 24 * max(SHARES)), jnp.bfloat16),
+            pltpu.VMEM((3, SIDE, *grid, 2, rows, n), jnp.float32),
             pltpu.VMEM((3, 8, n), jnp.float32),
-            pltpu.VMEM((3, SIDE, *grid, 2, rows, n), jnp.int16),
-            pltpu.VMEM((3, SIDE, *grid, 2, rows, n), jnp.int16),
-            pltpu.VMEM((3, SIDE, *grid, 2, rows, n), jnp.int16),
         ]
+        + [pltpu.VMEM((3, SIDE, *grid, 2, rows, n), jnp.int16)] * 3
         + [sems((4,)), sems, sems((3, 4)), sems((3, 4))]
-        + exchange_sems * 2
-        + [sems((3, 4, 4))] * 2,
+        + [sems((3, 4, 4))] * (2 * len(SHARES))
+        + exchange_sems * (len(SHARES) + 1),
         compiler_params=pltpu.CompilerParams(
             collective_id=0, has_side_effects=True, vmem_limit_bytes=60 << 20
         ),

time: 147 us -> 137 us (0.932)
  Pallas kernels: 144 us -> 137 us
  local copies, waits for them, and re-layouts: 2.29 us -> 0 us
    pallas_call x1, Pallas kernels: 141 us -> 132 us  [cross(): pl.pallas_call(kernel, out_shape=[jax.ShapeDtypeStruct((3, SIDE, *grid, 2...]
    unnamed x4 -> x0, local copies, waits for them, and re-layouts: 2.29 us -> none
    pallas_call x1, Pallas kernels: 3.48 us -> 5.44 us  [decode(): pl.pallas_call(decode_kernel, grid=(rounds, 2), out_shape=jax.ShapeDtypeS...]
where the time goes in v5:
time: 137 us
  Pallas kernels  137 us (100%)
    pallas_call x1, Pallas kernels, cross(): pl.pallas_call(kernel, out_shape=[jax.ShapeDtypeStruct((3, SIDE, *grid, 2...  132 us
    pallas_call x1, Pallas kernels, decode(): pl.pallas_call(decode_kernel, grid=(rounds, 2), out_shape=jax.ShapeDtypeS...  5.44 us

profile of v5, /device:TPU:1, one launch (start us, length us, event | category | flops | bytes accessed | tf_op | source)
XLA Modules:
  0.0 137.0 jit_solution(8969353018334399534)
XLA Ops:
  0.0 131.6 %cross.1 = (s16[3,4,4,4,2,16,128]{6,5,4,3,2,1,0:T(8,128)(2,1)}, f32[3,4,4,4,1,128]{5,4,3,2,1,0:T(1,128)}) custom-call(s32[3,16]{1,0:T(4,128)} %mates.1, bf16[240,2,64,128]{3,2,1,0:T(8,128)(2,1)} %spectra.1), custom_call_target="tpu_custom_call" | custom-call | flops 6039797760 | bytes 16777216 | tf_op jit(solution)/shard_map/cross/pallas_call | solution.py:436
  131.6 5.4 %decode.1 = f32[3,1,16,2,64,128]{5,4,3,2,1,0:T(8,128)} custom-call(s16[3,64,2,16,128]{4,3,2,1,0:T(8,128)(2,1)} %bitcast.2, f32[3,64,1,128]{3,2,1,0:T(1,128)} %bitcast.3), custom_call_target="tpu_custom_call" | custom-call | tf_op jit(solution)/shard_map/decode/pallas_call | solution.py:416

commit v6 on v5

--- a/solution.py
+++ b/solution.py
@@ -190,12 +190,12 @@
                 continue
             load(j).wait()
 
-            @pl.loop(0, 2 * SIDE)
-            def turn(i):
-                q, x = i // SIDE, i % SIDE
-                v = stage[j % slots, :, q, pl.ds(pl.multiple_of(x * 16, 16), 16), :]
-                v = jnp.swapaxes(v, 0, 1).reshape(SIDE, SIDE, cut_rows, n)
-                ready[h][t, x, :, :, q, row : row + cut_rows, :] = v
+            @pl.loop(0, 2)
+            def turn(q):
+                for x in range(SIDE):
+                    v = stage[j % slots, :, q, x * 16 : (x + 1) * 16, :]
+                    v = jnp.swapaxes(v, 0, 1).reshape(SIDE, SIDE, cut_rows, n)
+                    ready[h][t, x, :, :, q, row : row + cut_rows, :] = v
 
             if j + slots < len(order):
                 load(j + slots).start()
@@ -299,7 +299,7 @@
         return 1.0 / jnp.broadcast_to(top, (1, n))
 
     for h in range(shares):
-        for thirds in ((0, 1), (2,)) if h == 0 else ((0, 1, 2),):
+        for thirds in ((0,), (1,), (2,)) if h == 0 else ((0, 1, 2),):
             relayout(h, thirds)
             if h == 0 and thirds[0] == 0:
                 pl.semaphore_wait(barrier, 10)
@@ -403,25 +403,50 @@
         copy.wait_send()
 
 
-def decode_kernel(codes, scales, o_ref):
-    n = codes.shape[-1]
-    share = codes[0, :, 0].astype(jnp.int32).astype(jnp.float32) * (1.0 / CODES)
-    value = share * share * (share * jnp.abs(share))
-    value = jnp.swapaxes(value, 0, 1)
-    o_ref[0, 0, :, 0] = value * scales[0].reshape(1, -1, n)
+def decode_kernel(codes, scales, o_ref, held, scale, value, held_sem, scale_sem, value_sem):
+    rounds, _, parts, _, n = held.shape
+    blocks = [(r, slice(None), pl.ds(q, 1)) for r in range(rounds) for q in range(parts)]
+    factors = pltpu.make_async_copy(scales, scale, scale_sem)
+    loads = [
+        pltpu.make_async_copy(codes.at[at], held.at[at], held_sem.at[k])
+        for k, at in enumerate(blocks)
+    ]
+    stores = [
+        pltpu.make_async_copy(value.at[at], o_ref.at[(at[0], 0, *at[1:])], value_sem.at[k])
+        for k, at in enumerate(blocks)
+    ]
+    factors.start()
+    for copy in loads:
+        copy.start()
+    factors.wait()
+    for k in range(len(blocks)):
+        r, q = k // parts, k % parts
+        loads[k].wait()
+        share = jnp.swapaxes(held[r, :, q], 0, 1)
+        share = share.astype(jnp.int32).astype(jnp.float32) * (1.0 / CODES)
+        root = share * share * (share * jnp.abs(share))
+        value[r, :, q] = root * scale[r].reshape(1, -1, n)
+        stores[k].start()
+    for copy in stores:
+        copy.wait()
 
 
 def decode(codes, scales):
-    rounds, f, _, rows, n = codes.shape
+    rounds, f, parts, rows, n = codes.shape
+    sems = pltpu.SemaphoreType.DMA
     return pl.pallas_call(
         decode_kernel,
-        grid=(rounds, 2),
-        out_shape=jax.ShapeDtypeStruct((rounds, 1, rows, 2, f, n), jnp.float32),
-        in_specs=[
-            pl.BlockSpec((1, f, 1, rows, n), lambda r, q: (r, 0, q, 0, 0)),
-            pl.BlockSpec((1, f, 1, n), lambda r, q: (r, 0, 0, 0)),
+        out_shape=jax.ShapeDtypeStruct((rounds, 1, rows, parts, f, n), jnp.float32),
+        in_specs=[pl.BlockSpec(memory_space=pl.ANY)] * 2,
+        out_specs=pl.BlockSpec(memory_space=pl.ANY),
+        scratch_shapes=[
+            pltpu.VMEM(codes.shape, codes.dtype),
+            pltpu.VMEM(scales.shape, scales.dtype),
+            pltpu.VMEM((rounds, rows, parts, f, n), jnp.float32),
+            sems((rounds * parts,)),
+            sems,
+            sems((rounds * parts,)),
         ],
-        out_specs=pl.BlockSpec((1, 1, rows, 1, f, n), lambda r, q: (r, 0, 0, q, 0, 0)),
         compiler_params=pltpu.CompilerParams(vmem_limit_bytes=60 << 20),
         name="decode",
     )(codes, scales)

time: 137 us -> 134 us (0.978)
  Pallas kernels: 137 us -> 134 us
    pallas_call x1, Pallas kernels: 5.44 us -> 3.6 us  [decode(): pl.pallas_call(decode_kernel, out_shape=jax.ShapeDtypeStruct((rounds, 1,...]
where the time goes in v6:
time: 134 us
  Pallas kernels  134 us (100%)
    pallas_call x1, Pallas kernels, cross(): pl.pallas_call(kernel, out_shape=[jax.ShapeDtypeStruct((3, SIDE, *grid, 2...  130 us
    pallas_call x1, Pallas kernels, decode(): pl.pallas_call(decode_kernel, out_shape=jax.ShapeDtypeStruct((rounds, 1,...  3.6 us

profile of v6, /device:TPU:1, one launch (start us, length us, event | category | flops | bytes accessed | tf_op | source)
XLA Modules:
  0.0 134.2 jit_solution(6063627547260335848)
XLA Ops:
  0.0 130.4 %cross.1 = (s16[3,4,4,4,2,16,128]{6,5,4,3,2,1,0:T(8,128)(2,1)}, f32[3,4,4,4,1,128]{5,4,3,2,1,0:T(1,128)}) custom-call(s32[3,16]{1,0:T(4,128)} %mates.1, bf16[240,2,64,128]{3,2,1,0:T(8,128)(2,1)} %spectra.1), custom_call_target="tpu_custom_call" | custom-call | flops 6039797760 | bytes 16777216 | tf_op jit(solution)/shard_map/cross/pallas_call | solution.py:461
  130.4 3.6 %decode.1 = f32[3,1,16,2,64,128]{5,4,3,2,1,0:T(8,128)} custom-call(s16[3,64,2,16,128]{4,3,2,1,0:T(8,128)(2,1)} %bitcast.2, f32[3,64,1,128]{3,2,1,0:T(1,128)} %bitcast.3), custom_call_target="tpu_custom_call" | custom-call | tf_op jit(solution)/shard_map/decode/pallas_call | solution.py:437

commit v7 on v6

--- a/solution.py
+++ b/solution.py
@@ -62,7 +62,7 @@
             device_id_type=MESH,
         )
         copy.start()
-        self.sent.append(copy)
+        self.sent.append((which, copy))
         return copy
 
     def keep(self, src, dst, which, at):
@@ -132,9 +132,11 @@
         else:
             copy.wait_recv()
 
-    def finish(self):
-        for copy in self.sent:
-            copy.wait_send()
+    def finish(self, before=3):
+        for which, copy in self.sent:
+            if which < before:
+                copy.wait_send()
+        self.sent = [(which, copy) for which, copy in self.sent if which >= before]
 
 
 def kernel(mates, spectra, o_ref, scales, *scratch):
@@ -147,6 +149,7 @@
 
     (stage,) = take(1)
     shares = len(SHARES)
+    last = shares - 1
     ready, first, second, every = take(shares), take(shares), take(shares), take(shares)
     turned, product, largest, part, first_out, second_out = take(6)
     stage_sem, scale_keep, scale_send, scale_recv = take(4)
@@ -255,11 +258,14 @@
             halves.append(jnp.concatenate(rows, axis=0))
         return jnp.concatenate(halves, axis=1)
 
+    def turn(h, i):
+        turned[i, :, : 24 * SHARES[h]] = wide(h, core, i % 2, i // 2).T
+
     def multiply(h, r, i):
         depth = 24 * SHARES[h]
         z, y_lo = i // 2, i % 2
-        if r == 0:
-            turned[i, :, :depth] = wide(h, core, y_lo, z).T
+        if r == 0 and h != last:
+            turn(h, i)
         mate = mates[r, i * 2 + core]
         g = jnp.dot(
             turned[i, :, :depth],
@@ -323,7 +329,6 @@
         for d2 in (0,) + STEPS:
             for t in range(3):
                 into[h].phase_three(t, d2)
-    last = shares - 1
     for d2 in (0,) + STEPS:
         swap(last - 1, d2)
     swapped(last - 1)
@@ -334,7 +339,9 @@
     products(last - 1, 2)
     swap(last, STEPS[1])
     swap(last, STEPS[2])
-    swapped(shares - 1)
+    for i in range(2 * SIDE):
+        turn(last, i)
+    swapped(last)
 
     scale = None
     for r in range(rounds + 1):
@@ -375,6 +382,10 @@
     kept.start()
     kept.wait()
     shared = scale_send_along(0)
+    for exchange in into:
+        exchange.finish()
+    for _, copy in swaps:
+        copy.wait_send()
     for d1 in STEPS:
         for t in range(3):
             back.arrive(back.one[t, d1], d1)
@@ -388,19 +399,18 @@
     for copy in shared[3:6]:
         copy.wait_recv()
     shared += scale_send_along(2)
+    for copy in shared[:6]:
+        copy.wait_send()
+    back.finish(2)
     for d2 in (0,) + STEPS:
         for d3 in (0,) + STEPS:
             for t in range(3):
                 back.arrive(back.three[t, d2, d3], d3)
     for copy in shared[6:]:
         copy.wait_recv()
-    for copy in shared:
+    for copy in shared[6:]:
         copy.wait_send()
-    for exchange in into:
-        exchange.finish()
     back.finish()
-    for _, copy in swaps:
-        copy.wait_send()
 
 
 def decode_kernel(codes, scales, o_ref, held, scale, value, held_sem, scale_sem, value_sem):

time: 134 us -> 133 us (level)
  Pallas kernels: 134 us -> 132 us
    pallas_call x1, Pallas kernels: 130 us -> 129 us  [cross(): pl.pallas_call(kernel, out_shape=[jax.ShapeDtypeStruct((3, SIDE, *grid, 2...]
where the time goes in v7:
time: 133 us; the launch traced here: 132 us
  Pallas kernels  132 us (99%)
    pallas_call x1, Pallas kernels, cross(): pl.pallas_call(kernel, out_shape=[jax.ShapeDtypeStruct((3, SIDE, *grid, 2...  129 us
    pallas_call x1, Pallas kernels, decode(): pl.pallas_call(decode_kernel, out_shape=jax.ShapeDtypeStruct((rounds, 1,...  3.6 us

profile of v7, /device:TPU:1, one launch (start us, length us, event | category | flops | bytes accessed | tf_op | source)
XLA Modules:
  0.0 132.4 jit_solution(4768034096959663208)
XLA Ops:
  0.0 128.7 %cross.1 = (s16[3,4,4,4,2,16,128]{6,5,4,3,2,1,0:T(8,128)(2,1)}, f32[3,4,4,4,1,128]{5,4,3,2,1,0:T(1,128)}) custom-call(s32[3,16]{1,0:T(4,128)} %mates.1, bf16[240,2,64,128]{3,2,1,0:T(8,128)(2,1)} %spectra.1), custom_call_target="tpu_custom_call" | custom-call | flops 6039797760 | bytes 16777216 | tf_op jit(solution)/shard_map/cross/pallas_call | solution.py:471
  128.7 3.6 %decode.1 = f32[3,1,16,2,64,128]{5,4,3,2,1,0:T(8,128)} custom-call(s16[3,64,2,16,128]{4,3,2,1,0:T(8,128)(2,1)} %bitcast.2, f32[3,64,1,128]{3,2,1,0:T(1,128)} %bitcast.3), custom_call_target="tpu_custom_call" | custom-call | tf_op jit(solution)/shard_map/decode/pallas_call | solution.py:447

commit v8 on v7

--- a/solution.py
+++ b/solution.py
@@ -261,11 +261,15 @@
     def turn(h, i):
         turned[i, :, : 24 * SHARES[h]] = wide(h, core, i % 2, i // 2).T
 
+    def turn_all(h):
+        @pl.loop(0, 2)
+        def blocks(j):
+            for k in range(SIDE):
+                turn(h, j * SIDE + k)
+
     def multiply(h, r, i):
         depth = 24 * SHARES[h]
         z, y_lo = i // 2, i % 2
-        if r == 0 and h != last:
-            turn(h, i)
         mate = mates[r, i * 2 + core]
         g = jnp.dot(
             turned[i, :, :depth],
@@ -323,6 +327,7 @@
         if h >= 2:
             for d2 in (0,) + STEPS:
                 swap(h - 2, d2)
+            turn_all(h - 2)
             swapped(h - 2)
             for r in range(rounds):
                 products(h - 2, r)
@@ -331,6 +336,7 @@
                 into[h].phase_three(t, d2)
     for d2 in (0,) + STEPS:
         swap(last - 1, d2)
+    turn_all(last - 1)
     swapped(last - 1)
     products(last - 1, 0)
     swap(last, 0)

time: 133 us -> 133 us (level)
  no operation moved by 1% of the time
where the time goes in v8:
time: 133 us; the launch traced here: 132 us
  Pallas kernels  132 us (99%)
    pallas_call x1, Pallas kernels, cross(): pl.pallas_call(kernel, out_shape=[jax.ShapeDtypeStruct((3, SIDE, *grid, 2...  128 us
    pallas_call x1, Pallas kernels, decode(): pl.pallas_call(decode_kernel, out_shape=jax.ShapeDtypeStruct((rounds, 1,...  3.6 us

profile of v8, /device:TPU:1, one launch (start us, length us, event | category | flops | bytes accessed | tf_op | source)
XLA Modules:
  0.0 131.8 jit_solution(18053452091606185194)
XLA Ops:
  0.0 128.0 %cross.1 = (s16[3,4,4,4,2,16,128]{6,5,4,3,2,1,0:T(8,128)(2,1)}, f32[3,4,4,4,1,128]{5,4,3,2,1,0:T(1,128)}) custom-call(s32[3,16]{1,0:T(4,128)} %mates.1, bf16[240,2,64,128]{3,2,1,0:T(8,128)(2,1)} %spectra.1), custom_call_target="tpu_custom_call" | custom-call | flops 6039797760 | bytes 16777216 | tf_op jit(solution)/shard_map/cross/pallas_call | solution.py:477
  128.0 3.6 %decode.1 = f32[3,1,16,2,64,128]{5,4,3,2,1,0:T(8,128)} custom-call(s16[3,64,2,16,128]{4,3,2,1,0:T(8,128)(2,1)} %bitcast.2, f32[3,64,1,128]{3,2,1,0:T(1,128)} %bitcast.3), custom_call_target="tpu_custom_call" | custom-call | tf_op jit(solution)/shard_map/decode/pallas_call | solution.py:453
